TPU v7x, 32 devices: a whole 2x2x4 slice. The times are simulated.
32 devices in a mesh: parts: 2 (over x), blk: 16 (over z, y, core).
Axes of the slice: x: 2, y: 2, z: 4, core: 2. Of those that a mesh axis runs over, the one named last changes fastest.
Arguments:
- small_emb: bfloat16 [8192, 768], P(('parts', 'blk')), parts along dimension 0
- small_cluster: int32 [8192], P(('parts', 'blk')), parts along dimension 0, may hold values from 0 to 255, as said below
- small_index: int32 [8192], P(('parts', 'blk')), parts along dimension 0, may hold values from 0 to 4095, each once
- big_emb: bfloat16 [16384, 768], P(('parts', 'blk')), parts along dimension 0
- big_cluster: int32 [16384], P(('parts', 'blk')), parts along dimension 0, may hold values from 0 to 1, as said below
- big_index: int32 [16384], P(('parts', 'blk')), parts along dimension 0, may hold values from 0 to 8191, each once
Outputs:
- small_best: float32 [8192], P(('parts', 'blk')), parts along dimension 0
- big_best: float32 [16384], P(('parts', 'blk')), parts along dimension 0
There are 2 independent parts, one for each index of `parts`. A program takes and returns all parts, laid end to end along the dimension named above; each array names one. Nothing has to cross between parts.
Inputs may be any that keep to these rules, and one draw needn't show every extreme that they name: `small_cluster`: on every device, at most 32 rows carry ids with one remainder on division by 16; on every device some remainder is held by exactly 32 rows, and one remainder is held by 32 rows on every device. `big_cluster`: rows on the devices with blk indices g * 16 to (g + 1) * 16 - 1 carry ids g * 2 to (g + 1) * 2 - 1.
All inputs are finite; a program needn't handle non-finite values.
Results may differ from a plain program's by a relative error of at most 0.00051.
Values may be sent and summed in bfloat16 or wider, within the bound.
A program may use at most 64 MiB of HBM per device.

v0:
```python
import jax
import jax.numpy as jnp
from jax import lax
from jax.sharding import PartitionSpec as P

CYCLE = 16


def shifted(block, axis, distance):
    devices = range(lax.axis_size(axis))
    route = [((i - distance) % len(devices), i) for i in devices]
    return lax.ppermute(block, axis, route)


def unit_rows(matrix):
    widened = matrix.astype(jnp.float32)
    scaled = widened * lax.rsqrt(jnp.sum(widened * widened, axis=1, keepdims=True) + 1e-06)
    return scaled.astype(jnp.bfloat16)


def update_best(best_sim, queries, query_ids, query_order, keys_in, key_ids, key_order):
    sim_grid = lax.dot_general(
        queries, keys_in, (((1,), (1,)), ((), ())), preferred_element_type=jnp.float32
    )
    keep_mask = (query_ids[:, None] == key_ids[None, :]) & (
        key_order[None, :] < query_order[:, None]
    )
    return jnp.maximum(best_sim, jnp.max(jnp.where(keep_mask, sim_grid, -1.0), axis=1))


def both_ways(own_best, carried, own_rows, own_ids, own_order, block_rows, block_ids, block_order):
    sim_grid = lax.dot_general(
        own_rows, block_rows, (((1,), (1,)), ((), ())), preferred_element_type=jnp.float32
    )
    same_id = own_ids[:, None] == block_ids[None, :]
    own_mask = same_id & (block_order[None, :] < own_order[:, None])
    block_mask = same_id & (own_order[:, None] < block_order[None, :])
    own_best = jnp.maximum(own_best, jnp.max(jnp.where(own_mask, sim_grid, -1.0), axis=1))
    carried = jnp.maximum(carried, jnp.max(jnp.where(block_mask, sim_grid, -1.0), axis=0))
    return (own_best, carried)


def on_device(small_emb, small_cluster, small_index, big_emb, big_cluster, big_index):
    devices = lax.axis_size("blk")
    row_count = small_emb.shape[0]
    width = small_emb.shape[1]
    capacity = 2 * row_count // devices
    small_unit = unit_rows(small_emb)
    owner_of = small_cluster % devices
    one_hot = (owner_of[:, None] == jnp.arange(devices, dtype=jnp.int32)[None, :]).astype(jnp.int32)
    earlier = jnp.cumsum(one_hot, axis=0) - one_hot
    rank_in = jnp.sum(earlier * one_hot, axis=1)
    slot_of = owner_of * capacity + rank_in
    send_rows = (
        jnp.zeros((devices * capacity, width), jnp.bfloat16)
        .at[slot_of]
        .set(small_unit)
        .reshape(devices, capacity, width)
    )
    send_ids = (
        jnp.full((devices * capacity,), -1, jnp.int32)
        .at[slot_of]
        .set(small_cluster)
        .reshape(devices, capacity)
    )
    send_order = (
        jnp.zeros((devices * capacity,), jnp.int32)
        .at[slot_of]
        .set(small_index)
        .reshape(devices, capacity)
    )
    got_rows, got_ids, got_order = (
        lax.all_to_all(send_rows, "blk", split_axis=0, concat_axis=0, tiled=True),
        lax.all_to_all(send_ids, "blk", split_axis=0, concat_axis=0, tiled=True),
        lax.all_to_all(send_order, "blk", split_axis=0, concat_axis=0, tiled=True),
    )
    flat_rows = got_rows.reshape(devices * capacity, width)
    flat_ids = got_ids.reshape(devices * capacity)
    flat_order = got_order.reshape(devices * capacity)
    start_best = jnp.full((devices * capacity,), -1.0, jnp.float32)
    owner_best = update_best(
        start_best, flat_rows, flat_ids, flat_order, flat_rows, flat_ids, flat_order
    )
    returned = lax.all_to_all(
        owner_best.reshape(devices, capacity), "blk", split_axis=0, concat_axis=0, tiled=True
    )
    small_best = returned.reshape(devices * capacity)[slot_of]
    big_unit = unit_rows(big_emb)
    best_sim = jnp.full((big_unit.shape[0],), -1.0, jnp.float32)
    best_sim = update_best(
        best_sim, big_unit, big_cluster, big_index, big_unit, big_cluster, big_index
    )
    carried_start = jnp.full((big_unit.shape[0],), -1.0, jnp.float32)

    def one_turn(step_num, carry):
        running, block_rows, block_ids, block_order, carried = carry
        block_rows, block_ids, block_order = shifted((block_rows, block_ids, block_order), "blk", 1)
        carried = shifted(carried, "blk", 1)
        running, carried = both_ways(
            running, carried, big_unit, big_cluster, big_index, block_rows, block_ids, block_order
        )
        return (running, block_rows, block_ids, block_order, carried)

    final = lax.fori_loop(
        0, CYCLE - 1, one_turn, (best_sim, big_unit, big_cluster, big_index, carried_start)
    )
    home_gap = shifted(1.0 - final[4], "blk", -(CYCLE - 1))
    best_sim = jnp.maximum(final[0], 1.0 - home_gap)
    return (small_best, best_sim)


def solution(mesh):
    placed = (
        P(("parts", "blk"), None),
        P(("parts", "blk")),
        P(("parts", "blk")),
        P(("parts", "blk"), None),
        P(("parts", "blk")),
        P(("parts", "blk")),
    )
    return jax.shard_map(
        on_device,
        mesh=mesh,
        in_specs=placed,
        out_specs=(P(("parts", "blk")), P(("parts", "blk"))),
        check_vma=False,
    )
```

profile of v0, /device:TPU:0, one launch (start us, length us, event | category | flops | bytes accessed | tf_op | source)
XLA Modules:
  0.0 296.9 jit_solution(8504994153312438417)
XLA Ops:
  5.9 7.4 %all-to-all-start = ((s32[16,1,32]{2,1,0:T(1,128)}), s32[16,1,32]{2,1,0:T(1,128)S(1)}, u32[]{:S(2)}, u32[]{:S(2)}) async-start(s32[16,1,32]{2,1,0:T(1,128)} %all_to_all.19), calls=%async_computation | async-start | bytes 16384 | tf_op jit(solution)/shard_map/all_to_all | solution.py:74
  19.7 5.1 %all-to-all-start.1 = ((s32[16,1,32]{2,1,0:T(1,128)}), s32[16,1,32]{2,1,0:T(1,128)S(1)}, u32[]{:S(2)}, u32[]{:S(2)}) async-start(s32[16,1,32]{2,1,0:T(1,128)} %all_to_all.21), calls=%async_computation.1 | async-start | bytes 16384 | tf_op jit(solution)/shard_map/all_to_all | solution.py:75
  24.9 2.7 scatter_custom_fusion.2
  27.6 3.6 %all-to-all-done.1 = s32[16,1,32]{2,1,0:T(1,128)S(1)} async-done(((s32[16,1,32]{2,1,0:T(1,128)}), s32[16,1,32]{2,1,0:T(1,128)S(1)}, u32[]{:S(2)}, u32[]{:S(2)}) %all-to-all-start.1) | async-done | bytes 2080 | tf_op jit(solution)/shard_map/all_to_all | solution.py:75
  31.2 3.6 %all-to-all-start.2 = ((bf16[16,32,768]{2,1,0:T(8,128)(2,1)}), bf16[16,32,768]{2,1,0:T(8,128)(2,1)S(1)}, u32[]{:S(2)}, u32[]{:S(2)}) async-start(bf16[16,32,768]{2,1,0:T(8,128)(2,1)} %bitcast.2), calls=%async_computation.2 | async-start | bytes 1572864 | tf_op jit(solution)/shard_map/all_to_all | solution.py:73
  34.9 242.6 %while.19 = (s32[]{:T(128)}, f32[512]{0:T(512)S(1)}, bf16[512,768]{1,0:T(8,128)(2,1)S(1)}, s32[512]{0:T(512)S(1)}, s32[512]{0:T(512)S(1)}, /*index=5*/f32[512]{0...) while((s32[]{:T(128)}, f32[512]{0:T(512)S(1)}, ...), condition=%wide.region_13.14_spmd.clone, body=%wide.region_10.13_spmd.clone.sunk | while | flops 405012992 | bytes 6353175 | solution.py:104
  38.4 23.6 %collective-permute-done.1 = s32[512]{0:T(512)S(1)} collective-permute-done((s32[512]{0:T(512)S(1)}, s32[512]{0:T(512)S(1)}, u32[]{:S(2)}, u32[]{:S(2)}) %collective-permute-start.1) | collective-permute-done | bytes 2080 | tf_op jit(solution)/shard_map/while/body/eval_jaxpr/ppermute | solution.py:12
  63.4 13.9 %collective-permute-done.1 = s32[512]{0:T(512)S(1)} collective-permute-done((s32[512]{0:T(512)S(1)}, s32[512]{0:T(512)S(1)}, u32[]{:S(2)}, u32[]{:S(2)}) %collective-permute-start.1) | collective-permute-done | bytes 2080 | tf_op jit(solution)/shard_map/while/body/eval_jaxpr/ppermute | solution.py:12
  78.7 13.9 %collective-permute-done.1 = s32[512]{0:T(512)S(1)} collective-permute-done((s32[512]{0:T(512)S(1)}, s32[512]{0:T(512)S(1)}, u32[]{:S(2)}, u32[]{:S(2)}) %collective-permute-start.1) | collective-permute-done | bytes 2080 | tf_op jit(solution)/shard_map/while/body/eval_jaxpr/ppermute | solution.py:12
  94.0 13.9 %collective-permute-done.1 = s32[512]{0:T(512)S(1)} collective-permute-done((s32[512]{0:T(512)S(1)}, s32[512]{0:T(512)S(1)}, u32[]{:S(2)}, u32[]{:S(2)}) %collective-permute-start.1) | collective-permute-done | bytes 2080 | tf_op jit(solution)/shard_map/while/body/eval_jaxpr/ppermute | solution.py:12
  109.3 13.9 %collective-permute-done.1 = s32[512]{0:T(512)S(1)} collective-permute-done((s32[512]{0:T(512)S(1)}, s32[512]{0:T(512)S(1)}, u32[]{:S(2)}, u32[]{:S(2)}) %collective-permute-start.1) | collective-permute-done | bytes 2080 | tf_op jit(solution)/shard_map/while/body/eval_jaxpr/ppermute | solution.py:12
  124.6 13.9 %collective-permute-done.1 = s32[512]{0:T(512)S(1)} collective-permute-done((s32[512]{0:T(512)S(1)}, s32[512]{0:T(512)S(1)}, u32[]{:S(2)}, u32[]{:S(2)}) %collective-permute-start.1) | collective-permute-done | bytes 2080 | tf_op jit(solution)/shard_map/while/body/eval_jaxpr/ppermute | solution.py:12
  139.9 13.9 %collective-permute-done.1 = s32[512]{0:T(512)S(1)} collective-permute-done((s32[512]{0:T(512)S(1)}, s32[512]{0:T(512)S(1)}, u32[]{:S(2)}, u32[]{:S(2)}) %collective-permute-start.1) | collective-permute-done | bytes 2080 | tf_op jit(solution)/shard_map/while/body/eval_jaxpr/ppermute | solution.py:12
  155.2 13.9 %collective-permute-done.1 = s32[512]{0:T(512)S(1)} collective-permute-done((s32[512]{0:T(512)S(1)}, s32[512]{0:T(512)S(1)}, u32[]{:S(2)}, u32[]{:S(2)}) %collective-permute-start.1) | collective-permute-done | bytes 2080 | tf_op jit(solution)/shard_map/while/body/eval_jaxpr/ppermute | solution.py:12
  170.5 13.9 %collective-permute-done.1 = s32[512]{0:T(512)S(1)} collective-permute-done((s32[512]{0:T(512)S(1)}, s32[512]{0:T(512)S(1)}, u32[]{:S(2)}, u32[]{:S(2)}) %collective-permute-start.1) | collective-permute-done | bytes 2080 | tf_op jit(solution)/shard_map/while/body/eval_jaxpr/ppermute | solution.py:12
  185.8 13.9 %collective-permute-done.1 = s32[512]{0:T(512)S(1)} collective-permute-done((s32[512]{0:T(512)S(1)}, s32[512]{0:T(512)S(1)}, u32[]{:S(2)}, u32[]{:S(2)}) %collective-permute-start.1) | collective-permute-done | bytes 2080 | tf_op jit(solution)/shard_map/while/body/eval_jaxpr/ppermute | solution.py:12
  201.2 13.9 %collective-permute-done.1 = s32[512]{0:T(512)S(1)} collective-permute-done((s32[512]{0:T(512)S(1)}, s32[512]{0:T(512)S(1)}, u32[]{:S(2)}, u32[]{:S(2)}) %collective-permute-start.1) | collective-permute-done | bytes 2080 | tf_op jit(solution)/shard_map/while/body/eval_jaxpr/ppermute | solution.py:12
  216.5 13.9 %collective-permute-done.1 = s32[512]{0:T(512)S(1)} collective-permute-done((s32[512]{0:T(512)S(1)}, s32[512]{0:T(512)S(1)}, u32[]{:S(2)}, u32[]{:S(2)}) %collective-permute-start.1) | collective-permute-done | bytes 2080 | tf_op jit(solution)/shard_map/while/body/eval_jaxpr/ppermute | solution.py:12
  231.8 13.9 %collective-permute-done.1 = s32[512]{0:T(512)S(1)} collective-permute-done((s32[512]{0:T(512)S(1)}, s32[512]{0:T(512)S(1)}, u32[]{:S(2)}, u32[]{:S(2)}) %collective-permute-start.1) | collective-permute-done | bytes 2080 | tf_op jit(solution)/shard_map/while/body/eval_jaxpr/ppermute | solution.py:12
  247.1 13.9 %collective-permute-done.1 = s32[512]{0:T(512)S(1)} collective-permute-done((s32[512]{0:T(512)S(1)}, s32[512]{0:T(512)S(1)}, u32[]{:S(2)}, u32[]{:S(2)}) %collective-permute-start.1) | collective-permute-done | bytes 2080 | tf_op jit(solution)/shard_map/while/body/eval_jaxpr/ppermute | solution.py:12
  262.4 13.9 %collective-permute-done.1 = s32[512]{0:T(512)S(1)} collective-permute-done((s32[512]{0:T(512)S(1)}, s32[512]{0:T(512)S(1)}, u32[]{:S(2)}, u32[]{:S(2)}) %collective-permute-start.1) | collective-permute-done | bytes 2080 | tf_op jit(solution)/shard_map/while/body/eval_jaxpr/ppermute | solution.py:12
  280.9 5.8 %all-to-all-start.3 = ((f32[16,1,32]{2,1,0:T(1,128)}), f32[16,1,32]{2,1,0:T(1,128)S(1)}, u32[]{:S(2)}, u32[]{:S(2)}) async-start(f32[16,1,32]{2,1,0:T(1,128)} %max_broadcast_in_dim.18), calls=%async_computation.3 | async-start | bytes 16384 | tf_op jit(solution)/shard_map/all_to_all | solution.py:84
  287.3 5.8 %all-to-all-done.3 = f32[16,1,32]{2,1,0:T(1,128)S(1)} async-done(((f32[16,1,32]{2,1,0:T(1,128)}), f32[16,1,32]{2,1,0:T(1,128)S(1)}, u32[]{:S(2)}, u32[]{:S(2)}) %all-to-all-start.3) | async-done | bytes 2080 | tf_op jit(solution)/shard_map/all_to_all | solution.py:84
  294.4 2.5 gather_fusion
  (260 shorter events, 39.8 us)
Async XLA Ops:
  31.2 248.3 %all-to-all-start.2 = ((bf16[16,32,768]{2,1,0:T(8,128)(2,1)}), bf16[16,32,768]{2,1,0:T(8,128)(2,1)S(1)}, u32[]{:S(2)}, u32[]{:S(2)}) async-start(bf16[16,32,768]{2,1,0:T(8,128)(2,1)} %bitcast.2), calls=%async_computation.2 | async-start | bytes 1572864 | tf_op jit(solution)/shard_map/all_to_all | solution.py:73
  34.9 27.1 %collective-permute-start.2 = (bf16[512,768]{1,0:T(8,128)(2,1)S(1)}, bf16[512,768]{1,0:T(8,128)(2,1)S(1)}, u32[]{:S(2)}, u32[]{:S(2)}) collective-permute-start(bf16[512,768]{1,0:T(8,128)(2,1)S(1)} %get-tuple-element.174), channel_id=1, source_target_pairs={{15,0},{0,1},{1,2},{2,3},{3,4},{4,5},{5,6},{6,7},{7,8},{8,9},{9,10... | collective-permute-start | bytes 2359304 | tf_op jit(solution)/shard_map/while/body/eval_jaxpr/ppermute | solution.py:12
  35.2 26.8 %collective-permute-start = (s32[512]{0:T(512)S(1)}, s32[512]{0:T(512)S(1)}, u32[]{:S(2)}, u32[]{:S(2)}) collective-permute-start(s32[512]{0:T(512)S(1)} %get-tuple-element.176), channel_id=1, source_target_pairs={{15,0},{0,1},{1,2},{2,3},{3,4},{4,5},{5,6},{6,7},{7,8},{8,9},{9,10... | collective-permute-start | bytes 6152 | tf_op jit(solution)/shard_map/while/body/eval_jaxpr/ppermute | solution.py:12
  36.8 25.2 %collective-permute-start.1 = (s32[512]{0:T(512)S(1)}, s32[512]{0:T(512)S(1)}, u32[]{:S(2)}, u32[]{:S(2)}) collective-permute-start(s32[512]{0:T(512)S(1)} %get-tuple-element.175), channel_id=1, source_target_pairs={{15,0},{0,1},{1,2},{2,3},{3,4},{4,5},{5,6},{6,7},{7,8},{8,9},{9,10... | collective-permute-start | bytes 6152 | tf_op jit(solution)/shard_map/while/body/eval_jaxpr/ppermute | solution.py:12
  37.0 26.1 %collective-permute-start.3 = (f32[512]{0:T(512)S(1)}, f32[512]{0:T(512)S(1)}, u32[]{:S(2)}, u32[]{:S(2)}) collective-permute-start(f32[512]{0:T(512)S(1)} %broadcast_select_fusion.2), channel_id=1, source_target_pairs={{15,0},{0,1},{1,2},{2,3},{3,4},{4,5},{5,6},{6,7},{7,8},{8,9},{9,10... | collective-permute-start | bytes 6152 | tf_op jit(solution)/shard_map/while/body/eval_jaxpr/ppermute | solution.py:12
  63.1 14.2 %collective-permute-start.2 = (bf16[512,768]{1,0:T(8,128)(2,1)S(1)}, bf16[512,768]{1,0:T(8,128)(2,1)S(1)}, u32[]{:S(2)}, u32[]{:S(2)}) collective-permute-start(bf16[512,768]{1,0:T(8,128)(2,1)S(1)} %get-tuple-element.174), channel_id=1, source_target_pairs={{15,0},{0,1},{1,2},{2,3},{3,4},{4,5},{5,6},{6,7},{7,8},{8,9},{9,10... | collective-permute-start | bytes 2359304 | tf_op jit(solution)/shard_map/while/body/eval_jaxpr/ppermute | solution.py:12
  63.3 15.1 %collective-permute-start.3 = (f32[512]{0:T(512)S(1)}, f32[512]{0:T(512)S(1)}, u32[]{:S(2)}, u32[]{:S(2)}) collective-permute-start(f32[512]{0:T(512)S(1)} %broadcast_select_fusion.2), channel_id=1, source_target_pairs={{15,0},{0,1},{1,2},{2,3},{3,4},{4,5},{5,6},{6,7},{7,8},{8,9},{9,10... | collective-permute-start | bytes 6152 | tf_op jit(solution)/shard_map/while/body/eval_jaxpr/ppermute | solution.py:12
  78.4 14.2 %collective-permute-start.2 = (bf16[512,768]{1,0:T(8,128)(2,1)S(1)}, bf16[512,768]{1,0:T(8,128)(2,1)S(1)}, u32[]{:S(2)}, u32[]{:S(2)}) collective-permute-start(bf16[512,768]{1,0:T(8,128)(2,1)S(1)} %get-tuple-element.174), channel_id=1, source_target_pairs={{15,0},{0,1},{1,2},{2,3},{3,4},{4,5},{5,6},{6,7},{7,8},{8,9},{9,10... | collective-permute-start | bytes 2359304 | tf_op jit(solution)/shard_map/while/body/eval_jaxpr/ppermute | solution.py:12
  78.6 15.1 %collective-permute-start.3 = (f32[512]{0:T(512)S(1)}, f32[512]{0:T(512)S(1)}, u32[]{:S(2)}, u32[]{:S(2)}) collective-permute-start(f32[512]{0:T(512)S(1)} %broadcast_select_fusion.2), channel_id=1, source_target_pairs={{15,0},{0,1},{1,2},{2,3},{3,4},{4,5},{5,6},{6,7},{7,8},{8,9},{9,10... | collective-permute-start | bytes 6152 | tf_op jit(solution)/shard_map/while/body/eval_jaxpr/ppermute | solution.py:12
  93.7 14.2 %collective-permute-start.2 = (bf16[512,768]{1,0:T(8,128)(2,1)S(1)}, bf16[512,768]{1,0:T(8,128)(2,1)S(1)}, u32[]{:S(2)}, u32[]{:S(2)}) collective-permute-start(bf16[512,768]{1,0:T(8,128)(2,1)S(1)} %get-tuple-element.174), channel_id=1, source_target_pairs={{15,0},{0,1},{1,2},{2,3},{3,4},{4,5},{5,6},{6,7},{7,8},{8,9},{9,10... | collective-permute-start | bytes 2359304 | tf_op jit(solution)/shard_map/while/body/eval_jaxpr/ppermute | solution.py:12
  93.9 15.1 %collective-permute-start.3 = (f32[512]{0:T(512)S(1)}, f32[512]{0:T(512)S(1)}, u32[]{:S(2)}, u32[]{:S(2)}) collective-permute-start(f32[512]{0:T(512)S(1)} %broadcast_select_fusion.2), channel_id=1, source_target_pairs={{15,0},{0,1},{1,2},{2,3},{3,4},{4,5},{5,6},{6,7},{7,8},{8,9},{9,10... | collective-permute-start | bytes 6152 | tf_op jit(solution)/shard_map/while/body/eval_jaxpr/ppermute | solution.py:12
  109.0 14.2 %collective-permute-start.2 = (bf16[512,768]{1,0:T(8,128)(2,1)S(1)}, bf16[512,768]{1,0:T(8,128)(2,1)S(1)}, u32[]{:S(2)}, u32[]{:S(2)}) collective-permute-start(bf16[512,768]{1,0:T(8,128)(2,1)S(1)} %get-tuple-element.174), channel_id=1, source_target_pairs={{15,0},{0,1},{1,2},{2,3},{3,4},{4,5},{5,6},{6,7},{7,8},{8,9},{9,10... | collective-permute-start | bytes 2359304 | tf_op jit(solution)/shard_map/while/body/eval_jaxpr/ppermute | solution.py:12
  109.2 15.1 %collective-permute-start.3 = (f32[512]{0:T(512)S(1)}, f32[512]{0:T(512)S(1)}, u32[]{:S(2)}, u32[]{:S(2)}) collective-permute-start(f32[512]{0:T(512)S(1)} %broadcast_select_fusion.2), channel_id=1, source_target_pairs={{15,0},{0,1},{1,2},{2,3},{3,4},{4,5},{5,6},{6,7},{7,8},{8,9},{9,10... | collective-permute-start | bytes 6152 | tf_op jit(solution)/shard_map/while/body/eval_jaxpr/ppermute | solution.py:12
  124.3 14.2 %collective-permute-start.2 = (bf16[512,768]{1,0:T(8,128)(2,1)S(1)}, bf16[512,768]{1,0:T(8,128)(2,1)S(1)}, u32[]{:S(2)}, u32[]{:S(2)}) collective-permute-start(bf16[512,768]{1,0:T(8,128)(2,1)S(1)} %get-tuple-element.174), channel_id=1, source_target_pairs={{15,0},{0,1},{1,2},{2,3},{3,4},{4,5},{5,6},{6,7},{7,8},{8,9},{9,10... | collective-permute-start | bytes 2359304 | tf_op jit(solution)/shard_map/while/body/eval_jaxpr/ppermute | solution.py:12
  124.5 15.1 %collective-permute-start.3 = (f32[512]{0:T(512)S(1)}, f32[512]{0:T(512)S(1)}, u32[]{:S(2)}, u32[]{:S(2)}) collective-permute-start(f32[512]{0:T(512)S(1)} %broadcast_select_fusion.2), channel_id=1, source_target_pairs={{15,0},{0,1},{1,2},{2,3},{3,4},{4,5},{5,6},{6,7},{7,8},{8,9},{9,10... | collective-permute-start | bytes 6152 | tf_op jit(solution)/shard_map/while/body/eval_jaxpr/ppermute | solution.py:12
  139.8 15.1 %collective-permute-start.3 = (f32[512]{0:T(512)S(1)}, f32[512]{0:T(512)S(1)}, u32[]{:S(2)}, u32[]{:S(2)}) collective-permute-start(f32[512]{0:T(512)S(1)} %broadcast_select_fusion.2), channel_id=1, source_target_pairs={{15,0},{0,1},{1,2},{2,3},{3,4},{4,5},{5,6},{6,7},{7,8},{8,9},{9,10... | collective-permute-start | bytes 6152 | tf_op jit(solution)/shard_map/while/body/eval_jaxpr/ppermute | solution.py:12
  155.2 15.1 %collective-permute-start.3 = (f32[512]{0:T(512)S(1)}, f32[512]{0:T(512)S(1)}, u32[]{:S(2)}, u32[]{:S(2)}) collective-permute-start(f32[512]{0:T(512)S(1)} %broadcast_select_fusion.2), channel_id=1, source_target_pairs={{15,0},{0,1},{1,2},{2,3},{3,4},{4,5},{5,6},{6,7},{7,8},{8,9},{9,10... | collective-permute-start | bytes 6152 | tf_op jit(solution)/shard_map/while/body/eval_jaxpr/ppermute | solution.py:12
  170.5 15.1 %collective-permute-start.3 = (f32[512]{0:T(512)S(1)}, f32[512]{0:T(512)S(1)}, u32[]{:S(2)}, u32[]{:S(2)}) collective-permute-start(f32[512]{0:T(512)S(1)} %broadcast_select_fusion.2), channel_id=1, source_target_pairs={{15,0},{0,1},{1,2},{2,3},{3,4},{4,5},{5,6},{6,7},{7,8},{8,9},{9,10... | collective-permute-start | bytes 6152 | tf_op jit(solution)/shard_map/while/body/eval_jaxpr/ppermute | solution.py:12
  185.8 15.1 %collective-permute-start.3 = (f32[512]{0:T(512)S(1)}, f32[512]{0:T(512)S(1)}, u32[]{:S(2)}, u32[]{:S(2)}) collective-permute-start(f32[512]{0:T(512)S(1)} %broadcast_select_fusion.2), channel_id=1, source_target_pairs={{15,0},{0,1},{1,2},{2,3},{3,4},{4,5},{5,6},{6,7},{7,8},{8,9},{9,10... | collective-permute-start | bytes 6152 | tf_op jit(solution)/shard_map/while/body/eval_jaxpr/ppermute | solution.py:12
  201.1 15.1 %collective-permute-start.3 = (f32[512]{0:T(512)S(1)}, f32[512]{0:T(512)S(1)}, u32[]{:S(2)}, u32[]{:S(2)}) collective-permute-start(f32[512]{0:T(512)S(1)} %broadcast_select_fusion.2), channel_id=1, source_target_pairs={{15,0},{0,1},{1,2},{2,3},{3,4},{4,5},{5,6},{6,7},{7,8},{8,9},{9,10... | collective-permute-start | bytes 6152 | tf_op jit(solution)/shard_map/while/body/eval_jaxpr/ppermute | solution.py:12
  216.4 15.1 %collective-permute-start.3 = (f32[512]{0:T(512)S(1)}, f32[512]{0:T(512)S(1)}, u32[]{:S(2)}, u32[]{:S(2)}) collective-permute-start(f32[512]{0:T(512)S(1)} %broadcast_select_fusion.2), channel_id=1, source_target_pairs={{15,0},{0,1},{1,2},{2,3},{3,4},{4,5},{5,6},{6,7},{7,8},{8,9},{9,10... | collective-permute-start | bytes 6152 | tf_op jit(solution)/shard_map/while/body/eval_jaxpr/ppermute | solution.py:12
  231.7 15.1 %collective-permute-start.3 = (f32[512]{0:T(512)S(1)}, f32[512]{0:T(512)S(1)}, u32[]{:S(2)}, u32[]{:S(2)}) collective-permute-start(f32[512]{0:T(512)S(1)} %broadcast_select_fusion.2), channel_id=1, source_target_pairs={{15,0},{0,1},{1,2},{2,3},{3,4},{4,5},{5,6},{6,7},{7,8},{8,9},{9,10... | collective-permute-start | bytes 6152 | tf_op jit(solution)/shard_map/while/body/eval_jaxpr/ppermute | solution.py:12
  247.0 15.1 %collective-permute-start.3 = (f32[512]{0:T(512)S(1)}, f32[512]{0:T(512)S(1)}, u32[]{:S(2)}, u32[]{:S(2)}) collective-permute-start(f32[512]{0:T(512)S(1)} %broadcast_select_fusion.2), channel_id=1, source_target_pairs={{15,0},{0,1},{1,2},{2,3},{3,4},{4,5},{5,6},{6,7},{7,8},{8,9},{9,10... | collective-permute-start | bytes 6152 | tf_op jit(solution)/shard_map/while/body/eval_jaxpr/ppermute | solution.py:12
  262.3 15.1 %collective-permute-start.3 = (f32[512]{0:T(512)S(1)}, f32[512]{0:T(512)S(1)}, u32[]{:S(2)}, u32[]{:S(2)}) collective-permute-start(f32[512]{0:T(512)S(1)} %broadcast_select_fusion.2), channel_id=1, source_target_pairs={{15,0},{0,1},{1,2},{2,3},{3,4},{4,5},{5,6},{6,7},{7,8},{8,9},{9,10... | collective-permute-start | bytes 6152 | tf_op jit(solution)/shard_map/while/body/eval_jaxpr/ppermute | solution.py:12
  (45 other events, 586.3 us)
where the time goes:
time: 297 us
  waiting for transfers between devices  229 us (77%)
  starting transfers between devices  28.7 us (10%)
  matrix products  15.9 us (5%)
  local copies, waits for them, and re-layouts  10.8 us (4%)
  other arithmetic  10.3 us (3%)
    ppermute x61, waiting for transfers between devices, shifted(): return lax.ppermute(block, axis, route)  219 us
    dot_general x15, matrix products, both_ways(): lax.dot_general(own_rows, block_rows, (((1,), (1,)), ((), ())), preferred...  14.6 us
    all_to_all x1, starting transfers between devices, on_device(): lax.all_to_all(send_ids, 'blk', split_axis=0, concat_axis=0, tiled=True)  7.39 us
    ppermute x61, starting transfers between devices, shifted(): return lax.ppermute(block, axis, route)  6.86 us
  transfers between devices with their start and end apart: 65, of which 18 were waited for; matrix products, arithmetic and copies ran while one was open for 9% of the time, Pallas kernels for 0%

commit v1 on v0

--- a/solution.py
+++ b/solution.py
@@ -1,6 +1,8 @@
 import jax
 import jax.numpy as jnp
 from jax import lax
+from jax.experimental import pallas as pl
+from jax.experimental.pallas import tpu as pltpu
 from jax.sharding import PartitionSpec as P
 
 CYCLE = 16
@@ -109,6 +111,326 @@
     return (small_best, best_sim)
 
 
+MESH = pl.DeviceIdType.MESH
+META = 16
+COLS = 256
+
+
+class Side:
+    def __init__(self, flip, emb, meta, out, buf, rowid, rowor, colmeta, accr, accc, fin, ret, ss, rs, fs, frs):
+        self.emb, self.meta, self.out, self.buf = emb, meta, out, buf
+        self.rowid, self.rowor, self.colmeta = rowid, rowor, colmeta
+        self.accr, self.accc, self.fin, self.ret = accr, accc, fin, ret
+        self.ss, self.rs, self.fs, self.frs = ss, rs, fs, frs
+        self.flip = flip
+        self.rows = emb.shape[0]
+        self.parts = lax.axis_index("parts")
+        b = lax.axis_index("blk")
+        z = b // 4
+        self.level = 3 - z if flip else z
+        self.q = b % 4
+        self.y, self.c = self.q // 2, self.q % 2
+
+    def device(self, level, q):
+        z = 3 - level if self.flip else level
+        return (self.parts, z * 4 + q)
+
+    def copy(self, src, dst, dev, sem):
+        return pltpu.make_async_remote_copy(
+            src_ref=self.buf.at[src], dst_ref=self.buf.at[dst], send_sem=self.ss.at[sem],
+            recv_sem=self.rs.at[dst], device_id=dev, device_id_type=MESH,
+        )
+
+    def arrived(self, slot):
+        self.copy(slot, slot, self.device(self.level, self.q ^ 1), 0).wait_recv()
+
+    def plan(self):
+        site = self.level % 2 == 0
+        q, sib, opp = self.q, self.q ^ 1, self.q ^ 2
+        here = self.level
+        return {
+            0: (site, q, q, self.device(here, sib)),
+            1: (site, q, q, self.device(here, opp)),
+            2: (site, opp, opp, self.device(here, sib)),
+            3: (site, 4 + q, 4 + q, self.device(here, sib)),
+            4: (site, 4 + q, 4 + q, self.device(here, opp)),
+            5: (site, 4 + opp, 4 + opp, self.device(here, sib)),
+            6: (here == 0, q, 9, self.device(2, q)),
+            7: (here == 1, q, 8, self.device(2, q)),
+            8: (~site, q, 4 + q, self.device(here - 1, q)),
+        }
+
+    def send(self, sem):
+        cond, src, dst, dev = self.plan()[sem]
+
+        @pl.when(cond)
+        def _():
+            self.copy(src, dst, dev, sem).start()
+
+    def finish_sends(self):
+        for sem, (cond, src, dst, dev) in self.plan().items():
+
+            @pl.when(cond)
+            def _():
+                self.copy(src, dst, dev, sem).wait_send()
+
+    def prepare(self):
+        q = self.q
+        rows = self.rows
+
+        def step(t, _):
+            r = pl.multiple_of(t * 128, 128)
+            x = self.emb[pl.ds(r, 128), :].astype(jnp.float32)
+            s = x * lax.rsqrt(jnp.sum(x * x, axis=1, keepdims=True) + 1e-06)
+            self.buf[q, pl.ds(r, 128), :] = s.astype(jnp.bfloat16)
+            return 0
+
+        lax.fori_loop(0, rows // 128, step, 0)
+        self.buf[q, rows : rows + META, :] = self.meta[...]
+
+    def unpack(self, slot):
+        rows = self.rows
+        m = self.buf[slot, rows : rows + META, 0:rows].astype(jnp.float32)
+        ids = m[0:1] * 256.0 + m[1:2]
+        order = m[2:3] * 256.0 + m[3:4]
+        self.colmeta[slot, 0:8, :] = jnp.broadcast_to(ids, (8, rows))
+        self.colmeta[slot, 8:16, :] = jnp.broadcast_to(order, (8, rows))
+        self.rowid[slot] = jnp.broadcast_to(ids, (128, rows)).T
+        self.rowor[slot] = jnp.broadcast_to(order, (128, rows)).T
+        self.accr[slot] = jnp.full((rows, 128), -1.0, jnp.float32)
+        self.accc[slot] = jnp.full((8, rows), -1.0, jnp.float32)
+
+    def pair(self, i, j, both=True):
+        rows = self.rows
+        left = self.buf[i, 0:rows, :]
+        rid, ror = self.rowid[i], self.rowor[i]
+        best = self.accr[i]
+        for t in range(rows // COLS):
+            right = self.buf[j, t * COLS : (t + 1) * COLS, :]
+            sim = lax.dot_general(left, right, (((1,), (1,)), ((), ())), preferred_element_type=jnp.float32)
+            for g in range(COLS // 128):
+                at = t * COLS + g * 128
+                s = sim[:, g * 128 : (g + 1) * 128]
+                cid = self.colmeta[j, 0:1, at : at + 128]
+                cor = self.colmeta[j, 8:9, at : at + 128]
+                s = jnp.where(rid == cid, s, -1.0)
+                before = cor < ror
+                best = jnp.maximum(best, jnp.where(before, s, -1.0))
+                if both:
+                    back = jnp.where(before, -1.0, s).reshape(rows // 8, 8, 128)
+                    self.accc[j, :, at : at + 128] = jnp.maximum(
+                        self.accc[j, :, at : at + 128], jnp.max(back, axis=0)
+                    )
+        self.accr[i] = best
+
+    def pairs(self, count, index):
+        def step(n, _):
+            i, j = index(n)
+            self.pair(i, j)
+            return 0
+
+        lax.fori_loop(0, count, step, 0)
+
+    def site_work(self):
+        q, y, c = self.q, self.y, self.c
+        sib, opp, far = q ^ 1, q ^ 2, q ^ 3
+        crossed = self.level == 2
+        self.unpack(q)
+        self.pair(q, q, both=False)
+        self.arrived(sib)
+        self.unpack(sib)
+        self.arrived(opp)
+        self.send(2)
+        self.send(6)
+        self.arrived(4 + q)
+        self.send(3)
+        self.send(4)
+        self.unpack(opp)
+        self.unpack(4 + q)
+        self.pair(4 + q, 4 + q, both=False)
+        self.arrived(far)
+        self.unpack(far)
+        self.arrived(4 + sib)
+        self.unpack(4 + sib)
+
+        def early(n):
+            i = jnp.where(n < 2, q, c * 4 + q)
+            j = jnp.where(n == 0, 4 + q, jnp.where(n == 1, 4 + sib, c * 4 + sib))
+            return i, j
+
+        self.pairs(3, early)
+
+        @pl.when(crossed)
+        def _():
+            self.arrived(8)
+            self.unpack(8)
+            self.pairs(6, lambda n: (8, jnp.where(n < 4, n, 4 + y * 2 + (n - 4))))
+
+        self.arrived(4 + opp)
+        self.send(5)
+        self.unpack(4 + opp)
+        self.arrived(4 + far)
+        self.unpack(4 + far)
+
+        def late(n):
+            other = jnp.where(n % 2 == 0, opp, far)
+            i = jnp.where(n < 2, q, y * 4 + q)
+            j = jnp.where(n < 2, 4 + other, y * 4 + other)
+            return i, j
+
+        self.pairs(4, late)
+
+        @pl.when(crossed)
+        def _():
+            self.pairs(2, lambda n: (8, 4 + (1 - y) * 2 + n))
+            self.arrived(9)
+            self.unpack(9)
+            self.pairs(8, lambda n: (9, n))
+
+        def close(k, _):
+            self.close(k)
+
+            @pl.when(k != q)
+            def _():
+                self.back(k).start()
+
+            return 0
+
+        lax.fori_loop(0, 8, close, 0)
+
+        @pl.when(crossed)
+        def _():
+            for k in (8, 9):
+                self.close(k)
+                self.back_across(k).start()
+
+        self.ret[q] = self.fin[q]
+
+        def closed(k, _):
+            @pl.when(k != q)
+            def _():
+                self.back(k).wait_send()
+
+            return 0
+
+        lax.fori_loop(0, 8, closed, 0)
+
+        @pl.when(crossed)
+        def _():
+            for k in (8, 9):
+                self.back_across(k).wait_send()
+
+    def close(self, k):
+        flat = self.accr[k].T.reshape(16, 8, self.rows)
+        self.fin[k] = jnp.maximum(self.accc[k], jnp.max(flat, axis=0))
+
+    def back(self, k):
+        return self.back_to(k, self.q, self.device(self.level + k // 4, k % 4))
+
+    def back_across(self, k):
+        return self.back_to(k, 4, self.device(9 - k, self.q))
+
+    def back_to(self, k, place, dev):
+        return pltpu.make_async_remote_copy(
+            src_ref=self.fin.at[k], dst_ref=self.ret.at[place], send_sem=self.fs.at[k],
+            recv_sem=self.frs.at[place], device_id=dev, device_id_type=MESH,
+        )
+
+    def collect(self):
+        site = self.level % 2 == 0
+        first_half = self.level < 2
+
+        @pl.when(~first_half)
+        def _():
+            self.ret[4] = jnp.full((8, self.rows), -1.0, jnp.float32)
+
+        for p in range(4):
+
+            @pl.when(~(site & (self.q == p)))
+            def _():
+                self.back_to(p, p, self.device(self.level, self.q ^ 1)).wait_recv()
+
+        @pl.when(first_half)
+        def _():
+            self.back_to(4, 4, self.device(self.level, self.q ^ 1)).wait_recv()
+
+        best = self.ret[4]
+        for p in range(4):
+            best = jnp.maximum(best, self.ret[p])
+        self.out[...] = jnp.max(best, axis=0, keepdims=True)
+
+
+def grid_kernel(be, bm, se, sm, bo, so, *scratch):
+    half = len(scratch) // 2
+    big = Side(False, be, bm, bo, *scratch[:half])
+    small = Side(True, se, sm, so, *scratch[half:])
+    me = lax.axis_index("blk")
+    barrier = pltpu.get_barrier_semaphore()
+    for d in range(1, CYCLE):
+        peer = (big.parts, (me + d) % CYCLE)
+        pl.semaphore_signal(barrier, inc=1, device_id=peer, device_id_type=MESH)
+    big.prepare()
+    small.prepare()
+    pl.semaphore_wait(barrier, CYCLE - 1)
+    for side in (big, small):
+        side.send(0)
+        side.send(1)
+        side.send(7)
+        side.send(8)
+    for side in (big, small):
+        pl.when(side.level % 2 == 0)(side.site_work)
+    for side in (big, small):
+        side.collect()
+        side.finish_sends()
+
+
+def side_scratch(rows, width):
+    return [
+        pltpu.VMEM((10, rows + META, width), jnp.bfloat16),
+        pltpu.VMEM((10, rows, 128), jnp.float32),
+        pltpu.VMEM((10, rows, 128), jnp.float32),
+        pltpu.VMEM((10, 16, rows), jnp.float32),
+        pltpu.VMEM((10, rows, 128), jnp.float32),
+        pltpu.VMEM((10, 8, rows), jnp.float32),
+        pltpu.VMEM((10, 8, rows), jnp.float32),
+        pltpu.VMEM((5, 8, rows), jnp.float32),
+        pltpu.SemaphoreType.DMA((9,)),
+        pltpu.SemaphoreType.DMA((10,)),
+        pltpu.SemaphoreType.DMA((10,)),
+        pltpu.SemaphoreType.DMA((5,)),
+    ]
+
+
+def meta_rows(ids, order, width):
+    rows = jnp.stack([ids // 256, ids % 256, order // 256, order % 256])
+    return jnp.pad(rows, ((0, META - 4), (0, width - rows.shape[1]))).astype(jnp.bfloat16)
+
+
+def on_square_grid(small_emb, small_cluster, small_index, big_emb, big_cluster, big_index):
+    width = big_emb.shape[1]
+    big_rows, small_rows = big_emb.shape[0], small_emb.shape[0]
+    vmem = pl.BlockSpec(memory_space=pltpu.VMEM)
+    big_best, small_best = pl.pallas_call(
+        grid_kernel,
+        out_shape=(
+            jax.ShapeDtypeStruct((1, big_rows), jnp.float32),
+            jax.ShapeDtypeStruct((1, small_rows), jnp.float32),
+        ),
+        in_specs=[vmem] * 4,
+        out_specs=(vmem, vmem),
+        scratch_shapes=side_scratch(big_rows, width) + side_scratch(small_rows, width),
+        compiler_params=pltpu.CompilerParams(
+            collective_id=0, has_side_effects=True, vmem_limit_bytes=48 << 20
+        ),
+    )(
+        big_emb,
+        meta_rows(big_cluster, big_index, width),
+        small_emb,
+        meta_rows(small_cluster, small_index, width),
+    )
+    return (small_best.reshape(small_rows), big_best.reshape(big_rows))
+
+
 def solution(mesh):
     placed = (
         P(("parts", "blk"), None),
@@ -119,7 +441,7 @@
         P(("parts", "blk")),
     )
     return jax.shard_map(
-        on_device,
+        on_square_grid if mesh.shape["blk"] == CYCLE else on_device,
         mesh=mesh,
         in_specs=placed,
         out_specs=(P(("parts", "blk")), P(("parts", "blk"))),

time: 297 us -> 67.6 us (0.23)
  waiting for transfers between devices: 229 us -> 0 us
  Pallas kernels: 0 us -> 60.4 us
  starting transfers between devices: 28.7 us -> 0 us
  matrix products: 15.9 us -> 0 us
  other arithmetic: 10.3 us -> 0.76 us
  local copies, waits for them, and re-layouts: 10.8 us -> 5.29 us
    ppermute x61 -> x0, waiting for transfers between devices: 219 us -> none  [shifted(): return lax.ppermute(block, axis, route)]
    pallas_call x0 -> x1, Pallas kernels: none -> 60.4 us  [on_square_grid(): pl.pallas_call(grid_kernel, out_shape=(jax.ShapeDtypeStruct((1, big_rows)...]
    all_to_all x4 -> x0, starting transfers between devices: 21.9 us -> none  [the longest x1 7.39 us: on_device(): lax.all_to_all(send_ids, 'blk', split_axis=0, concat_axis=0, tiled=True)]
    dot_general x17 -> x0, matrix products: 15.9 us -> none  [the longest x15 14.6 us: both_ways(): lax.dot_general(own_rows, block_rows, (((1,), (1,)), ((), ())), preferred...]
    all_to_all x4 -> x0, waiting for transfers between devices: 10.4 us -> none  [the longest x1 5.81 us: on_device(): lax.all_to_all(owner_best.reshape(devices, capacity), 'blk', split_axis=0...]
    ppermute x61 -> x0, starting transfers between devices: 6.86 us -> none  [shifted(): return lax.ppermute(block, axis, route)]
    unnamed x11 -> x12, local copies, waits for them, and re-layouts: 0.88 us -> 5.25 us
    scatter x2 -> x0, local copies, waits for them, and re-layouts: 3.1 us -> none  [the longest x1 1.55 us: on_device(): send_order = jnp.zeros((devices * capacity,), jnp.int32).at[slot_of].set(...]
  transfers between devices with their start and end apart: 65 -> 0, of which waited for: 18 -> 0; matrix products, arithmetic and copies ran while one was open for 9% -> 0% of each run, Pallas kernels for 0% -> 0%
where the time goes in v1:
time: 67.6 us; the launch traced here: 67.2 us
  Pallas kernels  60.4 us (89%)
  local copies, waits for them, and re-layouts  5.29 us (8%)
  other arithmetic  0.76 us (1%)
  between operations  0.72 us (1%)
    pallas_call x1, Pallas kernels, on_square_grid(): pl.pallas_call(grid_kernel, out_shape=(jax.ShapeDtypeStruct((1, big_rows)...  60.4 us
    unnamed x12, local copies, waits for them, and re-layouts  5.25 us

profile of v1, /device:TPU:0, one launch (start us, length us, event | category | flops | bytes accessed | tf_op | source)
XLA Modules:
  0.0 67.2 jit_solution(6859289476585460362)
XLA Ops:
  0.6 0.7 %fusion.32 = (bf16[256]{0:T(256)(128)(2,1)S(1)}, bf16[256]{0:T(256)(128)(2,1)S(1)}) fusion(s32[256]{0:T(256)} %param.7), kind=kLoop, calls=%fused_computation.59 | loop fusion | flops 5376 | bytes 2048 | tf_op jit(solution)/shard_map/convert.9
  1.3 0.0 copy-start.4
  1.3 0.7 copy-done.4
  2.0 0.0 copy-start.2
  2.1 0.6 copy-done.2
  2.7 0.0 copy-start.3
  2.8 0.7 copy-done.3
  3.5 0.0 copy-start
  3.5 1.1 %copy-done = bf16[512,768]{1,0:T(8,128)(2,1)S(1)} copy-done((bf16[512,768]{1,0:T(8,128)(2,1)S(1)}, bf16[512,768]{1,0:T(8,128)(2,1)}, u32[]{:S(2)}) %copy-start) | copy-done | bytes 786456
  4.6 0.0 copy-start.1
  4.6 1.0 %copy-done.1 = bf16[256,768]{1,0:T(8,128)(2,1)S(1)} copy-done((bf16[256,768]{1,0:T(8,128)(2,1)S(1)}, bf16[256,768]{1,0:T(8,128)(2,1)}, u32[]{:S(2)}) %copy-start.1) | copy-done | bytes 393240
  5.6 60.4 %shard_map.77 = (f32[1,512]{1,0:T(1,128)S(1)}, f32[1,256]{1,0:T(1,128)S(1)}) custom-call(bf16[512,768]{1,0:T(8,128)(2,1)S(1)} %copy-done, bf16[16,768]{1,0:T(8,128)(2,1)S(1)} %get-tuple-element.14.bm, bf16[256,768]{1,0:T(8,128)(2,1)S(1)} %copy-done.1, bf16[16,768]{1,0:T(8,128)(2,1)S(1)} %get-tuple-element.15.sm), custom_call_target="tpu_custom_call" | custom-call | tf_op jit(solution)/shard_map/pallas_call | solution.py:413
  66.0 0.6 copy.10
  66.6 0.6 copy.11
  (12 shorter events, 0.1 us)
Async XLA Ops:
  1.3 0.7 %copy-start.4 = (s32[256]{0:T(256)S(1)}, s32[256]{0:T(256)}, u32[]{:S(2)}) copy-start(s32[256]{0:T(256)} %param.8) | copy-start | bytes 3076
  2.0 0.7 %copy-start.2 = (s32[512]{0:T(512)S(1)}, s32[512]{0:T(512)}, u32[]{:S(2)}) copy-start(s32[512]{0:T(512)} %param.10) | copy-start | bytes 6148
  2.7 0.7 %copy-start.3 = (s32[512]{0:T(512)S(1)}, s32[512]{0:T(512)}, u32[]{:S(2)}) copy-start(s32[512]{0:T(512)} %param.11) | copy-start | bytes 6148
  3.5 1.1 %copy-start = (bf16[512,768]{1,0:T(8,128)(2,1)S(1)}, bf16[512,768]{1,0:T(8,128)(2,1)}, u32[]{:S(2)}) copy-start(bf16[512,768]{1,0:T(8,128)(2,1)} %be.1) | copy-start | bytes 2359300
  4.6 1.0 %copy-start.1 = (bf16[256,768]{1,0:T(8,128)(2,1)S(1)}, bf16[256,768]{1,0:T(8,128)(2,1)}, u32[]{:S(2)}) copy-start(bf16[256,768]{1,0:T(8,128)(2,1)} %se.1) | copy-start | bytes 1179652

commit v2 on v1

--- a/solution.py
+++ b/solution.py
@@ -117,8 +117,9 @@
 
 
 class Side:
-    def __init__(self, flip, emb, meta, out, buf, rowid, rowor, colmeta, accr, accc, fin, ret, ss, rs, fs, frs):
-        self.emb, self.meta, self.out, self.buf = emb, meta, out, buf
+    def __init__(self, flip, hbm, out, emb, ids, order, ls, buf, rowid, rowor, colmeta, accr, accc, fin, ret, ss, rs, fs, frs):
+        self.hbm, self.loaded, self.ls, self.out, self.buf = hbm, (emb, ids, order), ls, out, buf
+        self.emb = emb
         self.rowid, self.rowor, self.colmeta = rowid, rowor, colmeta
         self.accr, self.accc, self.fin, self.ret = accr, accc, fin, ret
         self.ss, self.rs, self.fs, self.frs = ss, rs, fs, frs
@@ -174,9 +175,14 @@
             def _():
                 self.copy(src, dst, dev, sem).wait_send()
 
+    def loads(self):
+        return [pltpu.make_async_copy(h, v, self.ls.at[k]) for k, (h, v) in enumerate(zip(self.hbm, self.loaded))]
+
     def prepare(self):
         q = self.q
         rows = self.rows
+        for load in self.loads():
+            load.wait()
 
         def step(t, _):
             r = pl.multiple_of(t * 128, 128)
@@ -186,19 +192,28 @@
             return 0
 
         lax.fori_loop(0, rows // 128, step, 0)
-        self.buf[q, rows : rows + META, :] = self.meta[...]
-
-    def unpack(self, slot):
+        ids = jnp.broadcast_to(self.loaded[1][...].reshape(1, rows), (META, rows))
+        order = jnp.broadcast_to(self.loaded[2][...].reshape(1, rows), (META, rows))
+        line = lax.broadcasted_iota(jnp.int32, (META, rows), 0)
+        both = jnp.where(line < 2, ids, order)
+        digits = jnp.where(line % 2 == 0, both >> 8, both & 255)
+        digits = jnp.where(line < 4, digits, 0).astype(jnp.float32)
+        self.buf[q, rows : rows + META, 0:rows] = digits.astype(jnp.bfloat16)
+        self.buf[q, rows : rows + META, rows:] = jnp.zeros((META, self.buf.shape[2] - rows), jnp.bfloat16)
+
+    def unpack(self, slot, left=True):
         rows = self.rows
         m = self.buf[slot, rows : rows + META, 0:rows].astype(jnp.float32)
         ids = m[0:1] * 256.0 + m[1:2]
         order = m[2:3] * 256.0 + m[3:4]
         self.colmeta[slot, 0:8, :] = jnp.broadcast_to(ids, (8, rows))
         self.colmeta[slot, 8:16, :] = jnp.broadcast_to(order, (8, rows))
+        self.accc[slot] = jnp.full((8, rows), -1.0, jnp.float32)
+        if not left:
+            return
         self.rowid[slot] = jnp.broadcast_to(ids, (128, rows)).T
         self.rowor[slot] = jnp.broadcast_to(order, (128, rows)).T
         self.accr[slot] = jnp.full((rows, 128), -1.0, jnp.float32)
-        self.accc[slot] = jnp.full((8, rows), -1.0, jnp.float32)
 
     def pair(self, i, j, both=True):
         rows = self.rows
@@ -238,20 +253,20 @@
         self.unpack(q)
         self.pair(q, q, both=False)
         self.arrived(sib)
-        self.unpack(sib)
+        self.unpack(sib, left=False)
         self.arrived(opp)
         self.send(2)
         self.send(6)
         self.arrived(4 + q)
         self.send(3)
         self.send(4)
-        self.unpack(opp)
+        self.unpack(opp, left=False)
         self.unpack(4 + q)
         self.pair(4 + q, 4 + q, both=False)
         self.arrived(far)
-        self.unpack(far)
+        self.unpack(far, left=False)
         self.arrived(4 + sib)
-        self.unpack(4 + sib)
+        self.unpack(4 + sib, left=False)
 
         def early(n):
             i = jnp.where(n < 2, q, c * 4 + q)
@@ -268,9 +283,16 @@
 
         self.arrived(4 + opp)
         self.send(5)
-        self.unpack(4 + opp)
+        self.unpack(4 + opp, left=False)
+
+        @pl.when(crossed)
+        def _():
+            self.arrived(9)
+            self.unpack(9)
+            self.pairs(6, lambda n: (9, jnp.where(n < 4, n, 4 + y * 2 + (n - 4))))
+
         self.arrived(4 + far)
-        self.unpack(4 + far)
+        self.unpack(4 + far, left=False)
 
         def late(n):
             other = jnp.where(n % 2 == 0, opp, far)
@@ -282,13 +304,18 @@
 
         @pl.when(crossed)
         def _():
-            self.pairs(2, lambda n: (8, 4 + (1 - y) * 2 + n))
-            self.arrived(9)
-            self.unpack(9)
-            self.pairs(8, lambda n: (9, n))
+            self.pairs(4, lambda n: (8 + n // 2, 4 + (1 - y) * 2 + n % 2))
 
         def close(k, _):
-            self.close(k)
+            left = (k == q) | (k == 4 + q)
+
+            @pl.when(~left)
+            def _():
+                self.fin[k] = self.accc[k]
+
+            @pl.when(left)
+            def _():
+                self.close(k)
 
             @pl.when(k != q)
             def _():
@@ -357,26 +384,28 @@
         best = self.ret[4]
         for p in range(4):
             best = jnp.maximum(best, self.ret[p])
-        self.out[...] = jnp.max(best, axis=0, keepdims=True)
-
-
-def grid_kernel(be, bm, se, sm, bo, so, *scratch):
+        self.out[...] = jnp.max(best, axis=0)
+
+
+def grid_kernel(be, bc, bi, se, sc, si, bo, so, *scratch):
     half = len(scratch) // 2
-    big = Side(False, be, bm, bo, *scratch[:half])
-    small = Side(True, se, sm, so, *scratch[half:])
+    big = Side(False, (be, bc, bi), bo, *scratch[:half])
+    small = Side(True, (se, sc, si), so, *scratch[half:])
     me = lax.axis_index("blk")
     barrier = pltpu.get_barrier_semaphore()
     for d in range(1, CYCLE):
         peer = (big.parts, (me + d) % CYCLE)
         pl.semaphore_signal(barrier, inc=1, device_id=peer, device_id_type=MESH)
+    for side in (big, small):
+        for load in side.loads():
+            load.start()
     big.prepare()
+    pl.semaphore_wait(barrier, CYCLE - 1)
+    for sem in (8, 7, 1, 0):
+        big.send(sem)
     small.prepare()
-    pl.semaphore_wait(barrier, CYCLE - 1)
-    for side in (big, small):
-        side.send(0)
-        side.send(1)
-        side.send(7)
-        side.send(8)
+    for sem in (8, 7, 1, 0):
+        small.send(sem)
     for side in (big, small):
         pl.when(side.level % 2 == 0)(side.site_work)
     for side in (big, small):
@@ -386,6 +415,10 @@
 
 def side_scratch(rows, width):
     return [
+        pltpu.VMEM((rows, width), jnp.bfloat16),
+        pltpu.VMEM((rows,), jnp.int32),
+        pltpu.VMEM((rows,), jnp.int32),
+        pltpu.SemaphoreType.DMA((3,)),
         pltpu.VMEM((10, rows + META, width), jnp.bfloat16),
         pltpu.VMEM((10, rows, 128), jnp.float32),
         pltpu.VMEM((10, rows, 128), jnp.float32),
@@ -401,11 +434,6 @@
     ]
 
 
-def meta_rows(ids, order, width):
-    rows = jnp.stack([ids // 256, ids % 256, order // 256, order % 256])
-    return jnp.pad(rows, ((0, META - 4), (0, width - rows.shape[1]))).astype(jnp.bfloat16)
-
-
 def on_square_grid(small_emb, small_cluster, small_index, big_emb, big_cluster, big_index):
     width = big_emb.shape[1]
     big_rows, small_rows = big_emb.shape[0], small_emb.shape[0]
@@ -413,22 +441,17 @@
     big_best, small_best = pl.pallas_call(
         grid_kernel,
         out_shape=(
-            jax.ShapeDtypeStruct((1, big_rows), jnp.float32),
-            jax.ShapeDtypeStruct((1, small_rows), jnp.float32),
+            jax.ShapeDtypeStruct((big_rows,), jnp.float32),
+            jax.ShapeDtypeStruct((small_rows,), jnp.float32),
         ),
-        in_specs=[vmem] * 4,
+        in_specs=[pl.BlockSpec(memory_space=pl.ANY)] * 6,
         out_specs=(vmem, vmem),
         scratch_shapes=side_scratch(big_rows, width) + side_scratch(small_rows, width),
         compiler_params=pltpu.CompilerParams(
-            collective_id=0, has_side_effects=True, vmem_limit_bytes=48 << 20
+            collective_id=0, has_side_effects=True, vmem_limit_bytes=60 << 20
         ),
-    )(
-        big_emb,
-        meta_rows(big_cluster, big_index, width),
-        small_emb,
-        meta_rows(small_cluster, small_index, width),
-    )
-    return (small_best.reshape(small_rows), big_best.reshape(big_rows))
+    )(big_emb, big_cluster, big_index, small_emb, small_cluster, small_index)
+    return (small_best, big_best)
 
 
 def solution(mesh):

time: 67.6 us -> 62.6 us (0.926)
  local copies, waits for them, and re-layouts: 5.29 us -> 1.76 us
  other arithmetic: 0.76 us -> 0 us
    unnamed x12 -> x6, local copies, waits for them, and re-layouts: 5.25 us -> 1.76 us
    another operation x5 -> x0, other arithmetic: 0.76 us -> none
where the time goes in v2:
time: 62.6 us; the launch traced here: 62.5 us
  Pallas kernels  60 us (96%)
  local copies, waits for them, and re-layouts  1.76 us (3%)
  between operations  0.66 us (1%)
    pallas_call x1, Pallas kernels, on_square_grid(): pl.pallas_call(grid_kernel, out_shape=(jax.ShapeDtypeStruct((big_rows,),...  60 us
    unnamed x6, local copies, waits for them, and re-layouts  1.76 us

profile of v2, /device:TPU:0, one launch (start us, length us, event | category | flops | bytes accessed | tf_op | source)
XLA Modules:
  0.0 62.5 jit_solution(16530991722395963468)
XLA Ops:
  0.6 60.0 %shard_map.77 = (f32[512]{0:T(512)}, f32[256]{0:T(256)}) custom-call(bf16[512,768]{1,0:T(8,128)(2,1)} %be.1, s32[512]{0:T(512)} %bc.1, s32[512]{0:T(512)} %bi.1, bf16[256,768]{1,0:T(8,128)(2,1)} %se.1, s32[256]{0:T(256)} %sc.1, s32[256]{0:T(256)} %si.1), custom_call_target="tpu_custom_call" | custom-call | tf_op jit(solution)/shard_map/pallas_call | solution.py:441
  60.7 0.0 copy-start.1
  60.7 0.0 copy-start
  60.7 0.6 copy-done.1
  61.3 0.6 copy.10
  61.9 0.0 copy-done
  61.9 0.6 copy.11
Async XLA Ops:
  60.7 0.6 %copy-start.1 = (f32[256]{0:T(256)S(1)}, f32[256]{0:T(256)}, u32[]{:S(2)}) copy-start(f32[256]{0:T(256)} %get-tuple-element.8) | copy-start | bytes 3076
  60.7 1.2 %copy-start = (f32[512]{0:T(512)S(1)}, f32[512]{0:T(512)}, u32[]{:S(2)}) copy-start(f32[512]{0:T(512)} %get-tuple-element.9) | copy-start | bytes 6148

commit v3 on v2

--- a/solution.py
+++ b/solution.py
@@ -113,7 +113,7 @@
 
 MESH = pl.DeviceIdType.MESH
 META = 16
-COLS = 256
+COLS = 512
 
 
 class Side:
@@ -217,14 +217,15 @@
 
     def pair(self, i, j, both=True):
         rows = self.rows
+        cols = min(COLS, rows)
         left = self.buf[i, 0:rows, :]
         rid, ror = self.rowid[i], self.rowor[i]
         best = self.accr[i]
-        for t in range(rows // COLS):
-            right = self.buf[j, t * COLS : (t + 1) * COLS, :]
+        for t in range(rows // cols):
+            right = self.buf[j, t * cols : (t + 1) * cols, :]
             sim = lax.dot_general(left, right, (((1,), (1,)), ((), ())), preferred_element_type=jnp.float32)
-            for g in range(COLS // 128):
-                at = t * COLS + g * 128
+            for g in range(cols // 128):
+                at = t * cols + g * 128
                 s = sim[:, g * 128 : (g + 1) * 128]
                 cid = self.colmeta[j, 0:1, at : at + 128]
                 cor = self.colmeta[j, 8:9, at : at + 128]

time: 62.6 us -> 62.6 us (level)
  no operation moved by 1% of the time
where the time goes in v3:
time: 62.6 us; the launch traced here: 62.5 us
  Pallas kernels  60 us (96%)
  local copies, waits for them, and re-layouts  1.76 us (3%)
  between operations  0.66 us (1%)
    pallas_call x1, Pallas kernels, on_square_grid(): pl.pallas_call(grid_kernel, out_shape=(jax.ShapeDtypeStruct((big_rows,),...  60 us
    unnamed x6, local copies, waits for them, and re-layouts  1.76 us

profile of v3, /device:TPU:0, one launch (start us, length us, event | category | flops | bytes accessed | tf_op | source)
XLA Modules:
  0.0 62.5 jit_solution(16530991722395963468)
XLA Ops:
  0.6 60.0 %shard_map.77 = (f32[512]{0:T(512)}, f32[256]{0:T(256)}) custom-call(bf16[512,768]{1,0:T(8,128)(2,1)} %be.1, s32[512]{0:T(512)} %bc.1, s32[512]{0:T(512)} %bi.1, bf16[256,768]{1,0:T(8,128)(2,1)} %se.1, s32[256]{0:T(256)} %sc.1, s32[256]{0:T(256)} %si.1), custom_call_target="tpu_custom_call" | custom-call | tf_op jit(solution)/shard_map/pallas_call | solution.py:442
  60.7 0.0 copy-start.1
  60.7 0.0 copy-start
  60.7 0.6 copy-done.1
  61.3 0.6 copy.10
  61.9 0.0 copy-done
  61.9 0.6 copy.11
Async XLA Ops:
  60.7 0.6 %copy-start.1 = (f32[256]{0:T(256)S(1)}, f32[256]{0:T(256)}, u32[]{:S(2)}) copy-start(f32[256]{0:T(256)} %get-tuple-element.8) | copy-start | bytes 3076
  60.7 1.2 %copy-start = (f32[512]{0:T(512)S(1)}, f32[512]{0:T(512)}, u32[]{:S(2)}) copy-start(f32[512]{0:T(512)} %get-tuple-element.9) | copy-start | bytes 6148
